TPU v7x, 256 devices: a whole 4x4x8 slice. The times are simulated.
256 devices in a mesh: pb: 64 (over z, x, core), ka: 4 (over y).
Axes of the slice: x: 4, y: 4, z: 8, core: 2. Of those that a mesh axis runs over, the one named last changes fastest.
Arguments:
- queries: bfloat16 [65536, 512], P('pb'), may hold values from -80 to 80
- key_cache: bfloat16 [65536, 128], P(('ka', 'pb')), may hold values from -4.1 to 4.1
- value_cache: bfloat16 [65536, 128], P(('ka', 'pb')), may hold values from -4 to 4
- block_list: int32 [512, 32], P('pb'), may hold values from 0 to 511, as said below
- block_count: int32 [512], P('pb'), may hold values from 1 to 32, as said below
Outputs:
- attended: bfloat16 [65536, 512], P(('pb', 'ka'))
Inputs may be any that keep to these rules, and one draw needn't show every extreme that they name: `block_list`: entries of row qb before block_count[qb] are distinct blocks at most qb, and qb itself is among them. They are the blocks v at most qb of one set of 16 vertical blocks, then the blocks qb - o at least 0 (and not already listed) of one set of 16 slash offsets; both sets contain 0 and lie below 128. Later entries equal qb. `block_count`: the number of distinct listed blocks of each query block.
All inputs are finite; a program needn't handle non-finite values.
Results may differ from a plain program's by a relative error of at most 0.0046.
Values may be sent and summed in bfloat16 or wider, within the bound.
A program may use at most 128 MiB of HBM per device.

v0:
```python
import math
import jax
import jax.numpy as jnp
from jax import lax
from jax.sharding import PartitionSpec as P

HD = 128
QH = 4
BLK = 128
LIST = 32
masked_score = -1e30


def merged(shard, axis, combine):
    everything = jax.tree.map(lambda part: lax.all_gather(part, axis), shard)
    initial = jax.tree.map(lambda part: part[0], everything)

    def lap(k, so_far):
        return combine(so_far, jax.tree.map(lambda part: part[k], everything))

    return lax.fori_loop(1, lax.axis_size(axis), lap, initial)


def combine(first, second):
    peak_first, sum_first, out_first = first
    peak_second, sum_second, out_second = second
    peak_both = jnp.maximum(peak_first, peak_second)
    factor_first = jnp.exp(peak_first - peak_both)
    factor_second = jnp.exp(peak_second - peak_both)
    sum_both = factor_first * sum_first + factor_second * sum_second
    out_both = (
        jnp.repeat(factor_first, HD, axis=1) * out_first
        + jnp.repeat(factor_second, HD, axis=1) * out_second
    )
    return (peak_both, sum_both, out_both)


def shards(queries, key_cache, value_cache, block_list, block_count):
    shard_keys, shard_values = (
        lax.all_gather(key_cache, "pb", axis=0, tiled=True),
        lax.all_gather(value_cache, "pb", axis=0, tiled=True),
    )
    group_index = lax.axis_index("pb")
    shard_index = lax.axis_index("ka")
    ka_width = lax.axis_size("ka")
    score_scale = 1.0 / math.sqrt(HD)
    shard_width = shard_keys.shape[0] // BLK
    local_blocks = queries.shape[0] // BLK
    first_block = shard_index * shard_width
    all_key_tiles = shard_keys.reshape(shard_width, BLK, HD)
    all_value_tiles = shard_values.reshape(shard_width, BLK, HD)
    slot_ids = jnp.arange(LIST, dtype=jnp.int32)
    position = jnp.arange(BLK, dtype=jnp.int32)

    def one_block(block_pos):
        query_rows = lax.dynamic_slice_in_dim(queries, block_pos * BLK, BLK, 0).reshape(BLK, QH, HD)
        listed = lax.dynamic_index_in_dim(block_list, block_pos, 0, keepdims=False)
        live_count = lax.dynamic_index_in_dim(block_count, block_pos, 0, keepdims=False)
        global_pos = group_index * local_blocks + block_pos
        live_slot = slot_ids < live_count
        local_ids = listed - first_block
        tile_live = live_slot & (local_ids >= 0) & (local_ids < shard_width)
        picked = jnp.clip(local_ids, 0, shard_width - 1)
        key_tiles = all_key_tiles[picked]
        value_tiles = all_value_tiles[picked]
        scores = (
            jnp.einsum("qhd,skd->hqsk", query_rows, key_tiles, preferred_element_type=jnp.float32)
            * score_scale
        )
        earlier = (listed < global_pos)[None, :, None]
        diagonal = (listed == global_pos)[None, :, None] & (
            position[None, None, :] <= position[:, None, None]
        )
        valid = tile_live[None, :, None] & (earlier | diagonal)
        masked = jnp.where(valid[None], scores, masked_score)
        peak_row = jnp.max(masked, axis=(2, 3))
        weights = jnp.where(valid[None], jnp.exp(scores - peak_row[..., None, None]), 0.0)
        weight_sum = jnp.sum(weights, axis=(2, 3))
        partial_out = jnp.einsum(
            "hqsk,skd->qhd",
            weights.astype(jnp.bfloat16),
            value_tiles,
            preferred_element_type=jnp.float32,
        )
        return (peak_row.T, weight_sum.T, partial_out.reshape(BLK, QH * HD))

    peaks, sums, outputs = lax.map(one_block, jnp.arange(local_blocks, dtype=jnp.int32))
    peaks = peaks.reshape(local_blocks * BLK, QH)
    sums = sums.reshape(local_blocks * BLK, QH)
    outputs = outputs.reshape(local_blocks * BLK, QH * HD)
    merged_peak, merged_sum, merged_out = merged((peaks, sums, outputs), "ka", combine)
    owned = merged_out.shape[0] // ka_width
    out_share = lax.dynamic_slice_in_dim(merged_out, shard_index * owned, owned, 0)
    sum_share = lax.dynamic_slice_in_dim(merged_sum, shard_index * owned, owned, 0)
    return (out_share / jnp.repeat(sum_share, HD, axis=1)).astype(jnp.bfloat16)


def solution(mesh):
    placed = (P("pb", None), P(("ka", "pb"), None), P(("ka", "pb"), None), P("pb", None), P("pb"))
    return jax.shard_map(
        shards, mesh=mesh, in_specs=placed, out_specs=P(("pb", "ka"), None), check_vma=False
    )
```

profile of v0, /device:TPU:1, one launch (start us, length us, event | category | flops | bytes accessed | tf_op | source)
XLA Modules:
  0.0 492.1 jit_solution(4541151159910000270)
XLA Ops:
  8.1 85.3 %all-gather.4.cloned.1.call-done = bf16[16384,128]{1,0:T(8,128)(2,1)} async-done(((bf16[256,128]{1,0:T(8,128)(2,1)}), bf16[16384,128]{1,0:T(8,128)(2,1)}) %all-gather.4.cloned.1.call-update) | async-done | bytes 4194320 | tf_op jit(solution)/shard_map/all_gather | solution.py:40
  93.3 79.1 %all-gather.6.cloned.1.call-done = bf16[16384,128]{1,0:T(8,128)(2,1)} async-done(((bf16[256,128]{1,0:T(8,128)(2,1)}), bf16[16384,128]{1,0:T(8,128)(2,1)}) %all-gather.6.cloned.1.call-update) | async-done | bytes 4194320 | tf_op jit(solution)/shard_map/all_gather | solution.py:41
  172.4 201.8 %while.37 = (s32[]{:T(128)}, f32[8,128,4]{1,2,0:T(4,128)S(1)}, f32[8,128,4]{1,2,0:T(4,128)S(1)}, f32[8,128,512]{2,1,0:T(8,128)}, s32[8]{0:T(128)S(1)}, /*index=5...) while((s32[]{:T(128)}, f32[8,128,4]{1,2,0:T(4,128)S(1)}, ...), condition=%wide.region_3.4_spmd.clone, body=%wide.region_0.3_spmd.clone.sunk | while | flops 1098400256 | bytes 69129872 | solution.py:87
  181.2 2.9 gather_fusion
  191.6 5.2 %fusion.41 = f32[128,4,128,1]{2,0,1,3:T(8,128)S(1)} fusion(f32[32,128,128,4]{2,1,3,0:T(8,128)} %copy-done, f32[4,128]{1,0:T(4,128)S(1)} %get-tuple-element.581, pred[128,32,128]{0,2,1:T(8,128)(4,1)S(1)} %or_and_fusion.2, bf16[32,128,128]{2,1,0:T(8,128)(2,1)S(1)} %gather_fusion.1), kind=kOutput, calls=%fused_computation.20.clone.1 | convolution fusion | flops 545259520 | bytes 10225664 | tf_op jit(solution)/shard_map/while/body/eval_jaxpr/hqsk,skd->qhd/dot_general | solution.py:79
  206.4 2.9 gather_fusion
  216.8 5.2 %fusion.41 = f32[128,4,128,1]{2,0,1,3:T(8,128)S(1)} fusion(f32[32,128,128,4]{2,1,3,0:T(8,128)} %copy-done, f32[4,128]{1,0:T(4,128)S(1)} %get-tuple-element.581, pred[128,32,128]{0,2,1:T(8,128)(4,1)S(1)} %or_and_fusion.2, bf16[32,128,128]{2,1,0:T(8,128)(2,1)S(1)} %gather_fusion.1), kind=kOutput, calls=%fused_computation.20.clone.1 | convolution fusion | flops 545259520 | bytes 10225664 | tf_op jit(solution)/shard_map/while/body/eval_jaxpr/hqsk,skd->qhd/dot_general | solution.py:79
  231.7 2.9 gather_fusion
  242.0 5.2 %fusion.41 = f32[128,4,128,1]{2,0,1,3:T(8,128)S(1)} fusion(f32[32,128,128,4]{2,1,3,0:T(8,128)} %copy-done, f32[4,128]{1,0:T(4,128)S(1)} %get-tuple-element.581, pred[128,32,128]{0,2,1:T(8,128)(4,1)S(1)} %or_and_fusion.2, bf16[32,128,128]{2,1,0:T(8,128)(2,1)S(1)} %gather_fusion.1), kind=kOutput, calls=%fused_computation.20.clone.1 | convolution fusion | flops 545259520 | bytes 10225664 | tf_op jit(solution)/shard_map/while/body/eval_jaxpr/hqsk,skd->qhd/dot_general | solution.py:79
  267.2 5.2 %fusion.41 = f32[128,4,128,1]{2,0,1,3:T(8,128)S(1)} fusion(f32[32,128,128,4]{2,1,3,0:T(8,128)} %copy-done, f32[4,128]{1,0:T(4,128)S(1)} %get-tuple-element.581, pred[128,32,128]{0,2,1:T(8,128)(4,1)S(1)} %or_and_fusion.2, bf16[32,128,128]{2,1,0:T(8,128)(2,1)S(1)} %gather_fusion.1), kind=kOutput, calls=%fused_computation.20.clone.1 | convolution fusion | flops 545259520 | bytes 10225664 | tf_op jit(solution)/shard_map/while/body/eval_jaxpr/hqsk,skd->qhd/dot_general | solution.py:79
  282.1 2.9 gather_fusion
  292.4 5.2 %fusion.41 = f32[128,4,128,1]{2,0,1,3:T(8,128)S(1)} fusion(f32[32,128,128,4]{2,1,3,0:T(8,128)} %copy-done, f32[4,128]{1,0:T(4,128)S(1)} %get-tuple-element.581, pred[128,32,128]{0,2,1:T(8,128)(4,1)S(1)} %or_and_fusion.2, bf16[32,128,128]{2,1,0:T(8,128)(2,1)S(1)} %gather_fusion.1), kind=kOutput, calls=%fused_computation.20.clone.1 | convolution fusion | flops 545259520 | bytes 10225664 | tf_op jit(solution)/shard_map/while/body/eval_jaxpr/hqsk,skd->qhd/dot_general | solution.py:79
  307.3 2.9 gather_fusion
  317.7 5.2 %fusion.41 = f32[128,4,128,1]{2,0,1,3:T(8,128)S(1)} fusion(f32[32,128,128,4]{2,1,3,0:T(8,128)} %copy-done, f32[4,128]{1,0:T(4,128)S(1)} %get-tuple-element.581, pred[128,32,128]{0,2,1:T(8,128)(4,1)S(1)} %or_and_fusion.2, bf16[32,128,128]{2,1,0:T(8,128)(2,1)S(1)} %gather_fusion.1), kind=kOutput, calls=%fused_computation.20.clone.1 | convolution fusion | flops 545259520 | bytes 10225664 | tf_op jit(solution)/shard_map/while/body/eval_jaxpr/hqsk,skd->qhd/dot_general | solution.py:79
  342.9 5.2 %fusion.41 = f32[128,4,128,1]{2,0,1,3:T(8,128)S(1)} fusion(f32[32,128,128,4]{2,1,3,0:T(8,128)} %copy-done, f32[4,128]{1,0:T(4,128)S(1)} %get-tuple-element.581, pred[128,32,128]{0,2,1:T(8,128)(4,1)S(1)} %or_and_fusion.2, bf16[32,128,128]{2,1,0:T(8,128)(2,1)S(1)} %gather_fusion.1), kind=kOutput, calls=%fused_computation.20.clone.1 | convolution fusion | flops 545259520 | bytes 10225664 | tf_op jit(solution)/shard_map/while/body/eval_jaxpr/hqsk,skd->qhd/dot_general | solution.py:79
  368.1 5.2 %fusion.41 = f32[128,4,128,1]{2,0,1,3:T(8,128)S(1)} fusion(f32[32,128,128,4]{2,1,3,0:T(8,128)} %copy-done, f32[4,128]{1,0:T(4,128)S(1)} %get-tuple-element.581, pred[128,32,128]{0,2,1:T(8,128)(4,1)S(1)} %or_and_fusion.2, bf16[32,128,128]{2,1,0:T(8,128)(2,1)S(1)} %gather_fusion.1), kind=kOutput, calls=%fused_computation.20.clone.1 | convolution fusion | flops 545259520 | bytes 10225664 | tf_op jit(solution)/shard_map/while/body/eval_jaxpr/hqsk,skd->qhd/dot_general | solution.py:79
  374.2 9.6 %all_gather.17 = f32[4,1024,4]{1,2,0:T(4,128)S(1)} all-gather(f32[1,1024,4]{1,2,0:T(4,128)S(1)} %bitcast.155), channel_id=1, replica_groups=mesh['pb'=64,'ka'=4] {'ka'}, dimensions={0}, use_global_device_ids=true | all-gather | bytes 81920 | tf_op jit(solution)/shard_map/all_gather | solution.py:15
  383.8 9.9 %all_gather.18 = f32[4,1024,4]{1,2,0:T(4,128)S(1)} all-gather(f32[1,1024,4]{1,2,0:T(4,128)S(1)} %bitcast.156), channel_id=1, replica_groups=mesh['pb'=64,'ka'=4] {'ka'}, dimensions={0}, use_global_device_ids=true | all-gather | bytes 81920 | tf_op jit(solution)/shard_map/all_gather | solution.py:15
  393.7 63.6 %all-gather.8.cloned.1.call-done = f32[4,1024,512]{2,1,0:T(8,128)} async-done(((f32[1,1024,512]{2,1,0:T(8,128)}), f32[4,1024,512]{2,1,0:T(8,128)}) %all-gather.8.cloned.1.call-update) | async-done | bytes 8388624 | tf_op jit(solution)/shard_map/all_gather | solution.py:15
  457.3 3.1 slice_bitcast_fusion
  460.5 22.8 %while.36 = (s32[]{:T(128)}, f32[1024,4]{0,1:T(4,128)S(1)}, f32[1024,4]{0,1:T(4,128)S(1)}, f32[1024,512]{1,0:T(8,128)}, f32[4,1024,4]{1,2,0:T(4,128)S(1)}, /*ind...) while((s32[]{:T(128)}, f32[1024,4]{0,1:T(4,128)S(1)}, ...), condition=%wide.region_5.6_spmd, body=%wide.region_4.5_spmd.sunk | while | flops 1597445 | bytes 14909591 | solution.py:21
  463.4 4.6 fusion.34
  471.0 4.6 fusion.34
  478.6 4.6 fusion.34
  (186 shorter events, 132.0 us)
Async XLA Ops:
  6.5 86.8 %all-gather.4.cloned.1.call-start = ((), (), s32[]{:S(2)}) async-start(), calls=%async_computation | async-start | bytes 4259840 | tf_op jit(solution)/shard_map/all_gather | solution.py:40
  7.3 165.1 %all-gather.6.cloned.1.call-start = ((), (), s32[]{:S(2)}) async-start(), calls=%async_computation.1 | async-start | bytes 4259840 | tf_op jit(solution)/shard_map/all_gather | solution.py:41
  8.0 449.3 %all-gather.8.cloned.1.call-start = ((), (), s32[]{:S(2)}) async-start(), calls=%async_computation.2 | async-start | bytes 10485760 | tf_op jit(solution)/shard_map/all_gather | solution.py:15
  185.4 3.2 copy-start
  210.6 3.2 copy-start
  235.8 3.2 copy-start
  261.1 3.2 copy-start
  286.3 3.2 copy-start
  311.5 3.2 copy-start
  336.7 3.2 copy-start
  361.9 3.2 copy-start
Sparse Core Ops, SparseCore 0:
  10.1 83.1 all-gather.3
  96.1 76.2 all-gather.5
  374.3 82.9 all-gather.7
where the time goes:
time: 494 us; the launch traced here: 492 us
  waiting for transfers between devices  229 us (46%)
  local copies, waits for them, and re-layouts  101 us (20%)
  other arithmetic  51.8 us (10%)
  matrix products  51.4 us (10%)
  loops' own time  26.3 us (5%)
  blocking collectives  19.5 us (4%)
  between operations  13.1 us (3%)
    all_gather x1, waiting for transfers between devices, shards(): lax.all_gather(key_cache, 'pb', axis=0, tiled=True)  85.3 us
    all_gather x1, waiting for transfers between devices, shards(): lax.all_gather(value_cache, 'pb', axis=0, tiled=True)  79.1 us
    all_gather x1, waiting for transfers between devices, merged(): everything = jax.tree.map(lambda part: lax.all_gather(part, axis), shard)  63.6 us
    dot_general x8, matrix products, one_block(): jnp.einsum('hqsk,skd->qhd', weights.astype(jnp.bfloat16), value_tiles, pr...  41.5 us
    another operation x1, loops' own time, shards(): lax.map(one_block, jnp.arange(local_blocks, dtype=jnp.int32))  26.2 us
    gather x8, local copies, waits for them, and re-layouts, one_block(): key_tiles = all_key_tiles[picked]  23.5 us
    gather x8, local copies, waits for them, and re-layouts, one_block(): value_tiles = all_value_tiles[picked]  23.5 us
    all_gather x2, blocking collectives, merged(): everything = jax.tree.map(lambda part: lax.all_gather(part, axis), shard)  19.5 us
  transfers between devices with their start and end apart: 3, of which 3 were waited for; matrix products, arithmetic and copies ran while one was open for 0% of the time, Pallas kernels for 0%

commit v1 on v0

--- a/solution.py
+++ b/solution.py
@@ -36,9 +36,20 @@
 
 
 def shards(queries, key_cache, value_cache, block_list, block_count):
+
+    def test_meshes(sheet, device_axis, out_dim):
+        gallery = []
+        sides = lax.axis_size(device_axis)
+        for dd in range(sheet.ndim):
+            gallery.append(sides if dd == out_dim else 1)
+        heard = jnp.tile(sheet, gallery)
+        return lax.all_to_all(
+            heard, device_axis, concat_axis=out_dim, tiled=True, split_axis=out_dim
+        )
+
     shard_keys, shard_values = (
         lax.all_gather(key_cache, "pb", axis=0, tiled=True),
-        lax.all_gather(value_cache, "pb", axis=0, tiled=True),
+        test_meshes(value_cache, "pb", 0),
     )
     group_index = lax.axis_index("pb")
     shard_index = lax.axis_index("ka")

time: 494 us -> 449 us (0.909)
  waiting for transfers between devices: 229 us -> 173 us
  starting transfers between devices: 0.08 us -> 13.4 us
    all_gather x1 -> x0, waiting for transfers between devices: 79.1 us -> none  [shards(): lax.all_gather(value_cache, 'pb', axis=0, tiled=True)]
    all_to_all x0 -> x1, waiting for transfers between devices: none -> 16.6 us  [test_meshes(): lax.all_to_all(heard, device_axis, concat_axis=out_dim, tiled=True, split...]
    all_to_all x0 -> x1, starting transfers between devices: none -> 13.3 us  [test_meshes(): lax.all_to_all(heard, device_axis, concat_axis=out_dim, tiled=True, split...]
    dynamic_slice x8, local copies, waits for them, and re-layouts: 10.5 us -> 5.22 us  [one_block(): lax.dynamic_index_in_dim(block_count, block_pos, 0, keepdims=False)]
  transfers between devices with their start and end apart: 3 -> 3, of which waited for: 3 -> 3; matrix products, arithmetic and copies ran while one was open for 0% -> 1% of each run, Pallas kernels for 0% -> 0%
where the time goes in v1:
time: 449 us; the launch traced here: 447 us
  waiting for transfers between devices  173 us (39%)
  local copies, waits for them, and re-layouts  99.1 us (22%)
  other arithmetic  51.8 us (12%)
  matrix products  51.4 us (11%)
  loops' own time  26.3 us (6%)
  blocking collectives  19 us (4%)
  between operations  13.5 us (3%)
  starting transfers between devices  13.4 us (3%)
    all_gather x1, waiting for transfers between devices, shards(): lax.all_gather(key_cache, 'pb', axis=0, tiled=True)  90.1 us
    all_gather x1, waiting for transfers between devices, merged(): everything = jax.tree.map(lambda part: lax.all_gather(part, axis), shard)  65.2 us
    dot_general x8, matrix products, one_block(): jnp.einsum('hqsk,skd->qhd', weights.astype(jnp.bfloat16), value_tiles, pr...  41.5 us
    another operation x1, loops' own time, shards(): lax.map(one_block, jnp.arange(local_blocks, dtype=jnp.int32))  26.2 us
    gather x8, local copies, waits for them, and re-layouts, one_block(): key_tiles = all_key_tiles[picked]  23.5 us
    gather x8, local copies, waits for them, and re-layouts, one_block(): value_tiles = all_value_tiles[picked]  23.5 us
    all_gather x2, blocking collectives, merged(): everything = jax.tree.map(lambda part: lax.all_gather(part, axis), shard)  19 us
    all_to_all x1, waiting for transfers between devices, test_meshes(): lax.all_to_all(heard, device_axis, concat_axis=out_dim, tiled=True, split...  16.6 us
  transfers between devices with their start and end apart: 3, of which 3 were waited for; matrix products, arithmetic and copies ran while one was open for 1% of the time, Pallas kernels for 0%

profile of v1, /device:TPU:1, one launch (start us, length us, event | category | flops | bytes accessed | tf_op | source)
XLA Modules:
  0.0 446.9 jit_solution(2412707682118810137)
XLA Ops:
  7.3 3.8 tile.2
  11.1 13.3 %all-to-all-start = ((bf16[64,256,128]{2,1,0:T(8,128)(2,1)}), bf16[64,256,128]{2,1,0:T(8,128)(2,1)}, u32[]{:S(2)}, u32[]{:S(2)}) async-start(bf16[64,256,128]{2,1,0:T(8,128)(2,1)} %tile.2), calls=%async_computation | async-start | bytes 8388608 | tf_op jit(solution)/shard_map/all_to_all | solution.py:46
  24.5 90.1 %all-gather.3.cloned.1.call-done = bf16[16384,128]{1,0:T(8,128)(2,1)} async-done(((bf16[256,128]{1,0:T(8,128)(2,1)}), bf16[16384,128]{1,0:T(8,128)(2,1)}) %all-gather.3.cloned.1.call-update) | async-done | bytes 4194320 | tf_op jit(solution)/shard_map/all_gather | solution.py:51
  114.5 16.6 %all-to-all-done = bf16[64,256,128]{2,1,0:T(8,128)(2,1)} async-done(((bf16[64,256,128]{2,1,0:T(8,128)(2,1)}), bf16[64,256,128]{2,1,0:T(8,128)(2,1)}, u32[]{:S(2)}, u32[]{:S(2)}) %all-to-all-start) | async-done | bytes 4194336 | tf_op jit(solution)/shard_map/all_to_all | solution.py:46
  131.1 196.5 %while.37 = (s32[]{:T(128)}, f32[8,128,4]{1,2,0:T(4,128)S(1)}, f32[8,128,4]{1,2,0:T(4,128)S(1)}, f32[8,128,512]{2,1,0:T(8,128)}, s32[8]{0:T(128)S(1)}, /*index=5...) while((s32[]{:T(128)}, f32[8,128,4]{1,2,0:T(4,128)S(1)}, ...), condition=%wide.region_3.4_spmd.clone, body=%wide.region_0.3_spmd.clone.sunk | while | flops 1098400256 | bytes 69129872 | solution.py:98
  139.2 2.9 gather_fusion
  149.6 5.2 %fusion.41 = f32[128,4,128,1]{2,0,1,3:T(8,128)S(1)} fusion(f32[32,128,128,4]{2,1,3,0:T(8,128)} %copy-done, f32[4,128]{1,0:T(4,128)S(1)} %get-tuple-element.581, pred[128,32,128]{0,2,1:T(8,128)(4,1)S(1)} %or_and_fusion.2, bf16[32,128,128]{2,1,0:T(8,128)(2,1)S(1)} %gather_fusion.1), kind=kOutput, calls=%fused_computation.20.clone.1 | convolution fusion | flops 545259520 | bytes 10225664 | tf_op jit(solution)/shard_map/while/body/eval_jaxpr/hqsk,skd->qhd/dot_general | solution.py:90
  174.2 5.2 %fusion.41 = f32[128,4,128,1]{2,0,1,3:T(8,128)S(1)} fusion(f32[32,128,128,4]{2,1,3,0:T(8,128)} %copy-done, f32[4,128]{1,0:T(4,128)S(1)} %get-tuple-element.581, pred[128,32,128]{0,2,1:T(8,128)(4,1)S(1)} %or_and_fusion.2, bf16[32,128,128]{2,1,0:T(8,128)(2,1)S(1)} %gather_fusion.1), kind=kOutput, calls=%fused_computation.20.clone.1 | convolution fusion | flops 545259520 | bytes 10225664 | tf_op jit(solution)/shard_map/while/body/eval_jaxpr/hqsk,skd->qhd/dot_general | solution.py:90
  188.4 2.9 gather_fusion
  198.7 5.2 %fusion.41 = f32[128,4,128,1]{2,0,1,3:T(8,128)S(1)} fusion(f32[32,128,128,4]{2,1,3,0:T(8,128)} %copy-done, f32[4,128]{1,0:T(4,128)S(1)} %get-tuple-element.581, pred[128,32,128]{0,2,1:T(8,128)(4,1)S(1)} %or_and_fusion.2, bf16[32,128,128]{2,1,0:T(8,128)(2,1)S(1)} %gather_fusion.1), kind=kOutput, calls=%fused_computation.20.clone.1 | convolution fusion | flops 545259520 | bytes 10225664 | tf_op jit(solution)/shard_map/while/body/eval_jaxpr/hqsk,skd->qhd/dot_general | solution.py:90
  223.3 5.2 %fusion.41 = f32[128,4,128,1]{2,0,1,3:T(8,128)S(1)} fusion(f32[32,128,128,4]{2,1,3,0:T(8,128)} %copy-done, f32[4,128]{1,0:T(4,128)S(1)} %get-tuple-element.581, pred[128,32,128]{0,2,1:T(8,128)(4,1)S(1)} %or_and_fusion.2, bf16[32,128,128]{2,1,0:T(8,128)(2,1)S(1)} %gather_fusion.1), kind=kOutput, calls=%fused_computation.20.clone.1 | convolution fusion | flops 545259520 | bytes 10225664 | tf_op jit(solution)/shard_map/while/body/eval_jaxpr/hqsk,skd->qhd/dot_general | solution.py:90
  237.5 2.9 gather_fusion
  247.8 5.2 %fusion.41 = f32[128,4,128,1]{2,0,1,3:T(8,128)S(1)} fusion(f32[32,128,128,4]{2,1,3,0:T(8,128)} %copy-done, f32[4,128]{1,0:T(4,128)S(1)} %get-tuple-element.581, pred[128,32,128]{0,2,1:T(8,128)(4,1)S(1)} %or_and_fusion.2, bf16[32,128,128]{2,1,0:T(8,128)(2,1)S(1)} %gather_fusion.1), kind=kOutput, calls=%fused_computation.20.clone.1 | convolution fusion | flops 545259520 | bytes 10225664 | tf_op jit(solution)/shard_map/while/body/eval_jaxpr/hqsk,skd->qhd/dot_general | solution.py:90
  272.4 5.2 %fusion.41 = f32[128,4,128,1]{2,0,1,3:T(8,128)S(1)} fusion(f32[32,128,128,4]{2,1,3,0:T(8,128)} %copy-done, f32[4,128]{1,0:T(4,128)S(1)} %get-tuple-element.581, pred[128,32,128]{0,2,1:T(8,128)(4,1)S(1)} %or_and_fusion.2, bf16[32,128,128]{2,1,0:T(8,128)(2,1)S(1)} %gather_fusion.1), kind=kOutput, calls=%fused_computation.20.clone.1 | convolution fusion | flops 545259520 | bytes 10225664 | tf_op jit(solution)/shard_map/while/body/eval_jaxpr/hqsk,skd->qhd/dot_general | solution.py:90
  297.0 5.2 %fusion.41 = f32[128,4,128,1]{2,0,1,3:T(8,128)S(1)} fusion(f32[32,128,128,4]{2,1,3,0:T(8,128)} %copy-done, f32[4,128]{1,0:T(4,128)S(1)} %get-tuple-element.581, pred[128,32,128]{0,2,1:T(8,128)(4,1)S(1)} %or_and_fusion.2, bf16[32,128,128]{2,1,0:T(8,128)(2,1)S(1)} %gather_fusion.1), kind=kOutput, calls=%fused_computation.20.clone.1 | convolution fusion | flops 545259520 | bytes 10225664 | tf_op jit(solution)/shard_map/while/body/eval_jaxpr/hqsk,skd->qhd/dot_general | solution.py:90
  321.6 5.2 %fusion.41 = f32[128,4,128,1]{2,0,1,3:T(8,128)S(1)} fusion(f32[32,128,128,4]{2,1,3,0:T(8,128)} %copy-done, f32[4,128]{1,0:T(4,128)S(1)} %get-tuple-element.581, pred[128,32,128]{0,2,1:T(8,128)(4,1)S(1)} %or_and_fusion.2, bf16[32,128,128]{2,1,0:T(8,128)(2,1)S(1)} %gather_fusion.1), kind=kOutput, calls=%fused_computation.20.clone.1 | convolution fusion | flops 545259520 | bytes 10225664 | tf_op jit(solution)/shard_map/while/body/eval_jaxpr/hqsk,skd->qhd/dot_general | solution.py:90
  327.6 9.5 %all_gather.13 = f32[4,1024,4]{1,2,0:T(4,128)S(1)} all-gather(f32[1,1024,4]{1,2,0:T(4,128)S(1)} %bitcast.154), channel_id=1, replica_groups=mesh['pb'=64,'ka'=4] {'ka'}, dimensions={0}, use_global_device_ids=true | all-gather | bytes 81920 | tf_op jit(solution)/shard_map/all_gather | solution.py:15
  337.1 9.5 %all_gather.14 = f32[4,1024,4]{1,2,0:T(4,128)S(1)} all-gather(f32[1,1024,4]{1,2,0:T(4,128)S(1)} %bitcast.155), channel_id=1, replica_groups=mesh['pb'=64,'ka'=4] {'ka'}, dimensions={0}, use_global_device_ids=true | all-gather | bytes 81920 | tf_op jit(solution)/shard_map/all_gather | solution.py:15
  346.7 65.2 %all-gather.5.cloned.1.call-done = f32[4,1024,512]{2,1,0:T(8,128)} async-done(((f32[1,1024,512]{2,1,0:T(8,128)}), f32[4,1024,512]{2,1,0:T(8,128)}) %all-gather.5.cloned.1.call-update) | async-done | bytes 8388624 | tf_op jit(solution)/shard_map/all_gather | solution.py:15
  411.9 3.1 slice_bitcast_fusion
  415.0 22.8 %while.36 = (s32[]{:T(128)}, f32[1024,4]{0,1:T(4,128)S(1)}, f32[1024,4]{0,1:T(4,128)S(1)}, f32[1024,512]{1,0:T(8,128)}, f32[4,1024,4]{1,2,0:T(4,128)S(1)}, /*ind...) while((s32[]{:T(128)}, f32[1024,4]{0,1:T(4,128)S(1)}, ...), condition=%wide.region_5.6_spmd, body=%wide.region_4.5_spmd.sunk | while | flops 1597445 | bytes 14909591 | solution.py:21
  418.0 4.6 %fusion.34 = f32[1024,512]{1,0:T(8,128)} fusion(f32[128,8,4,128]{3,2,1,0:T(4,128)S(1)} %bitcast.147, f32[1024,512]{1,0:T(8,128)} %get-tuple-element.648, f32[128,8,4,128]{3,2,1,0:T(4,128)S(1)} %bitcast.148, f32[4,1024,512]{2,1,0:T(8,128)} %get-tuple-element.661, s32[]{:T(128)S(6)} %select_n.78), kind=kLoop, calls=%fused_computation.5.clone.1 | loop fusion | flops 1572864 | bytes 10485764 | tf_op jit(solution)/shard_map/while/body/eval_jaxpr/add | solution.py:32
  425.5 4.6 %fusion.34 = f32[1024,512]{1,0:T(8,128)} fusion(f32[128,8,4,128]{3,2,1,0:T(4,128)S(1)} %bitcast.147, f32[1024,512]{1,0:T(8,128)} %get-tuple-element.648, f32[128,8,4,128]{3,2,1,0:T(4,128)S(1)} %bitcast.148, f32[4,1024,512]{2,1,0:T(8,128)} %get-tuple-element.661, s32[]{:T(128)S(6)} %select_n.78), kind=kLoop, calls=%fused_computation.5.clone.1 | loop fusion | flops 1572864 | bytes 10485764 | tf_op jit(solution)/shard_map/while/body/eval_jaxpr/add | solution.py:32
  433.1 4.6 %fusion.34 = f32[1024,512]{1,0:T(8,128)} fusion(f32[128,8,4,128]{3,2,1,0:T(4,128)S(1)} %bitcast.147, f32[1024,512]{1,0:T(8,128)} %get-tuple-element.648, f32[128,8,4,128]{3,2,1,0:T(4,128)S(1)} %bitcast.148, f32[4,1024,512]{2,1,0:T(8,128)} %get-tuple-element.661, s32[]{:T(128)S(6)} %select_n.78), kind=kLoop, calls=%fused_computation.5.clone.1 | loop fusion | flops 1572864 | bytes 10485764 | tf_op jit(solution)/shard_map/while/body/eval_jaxpr/add | solution.py:32
  (188 shorter events, 132.0 us)
Async XLA Ops:
  6.5 108.0 %all-gather.3.cloned.1.call-start = ((), (), s32[]{:S(2)}) async-start(), calls=%async_computation.1 | async-start | bytes 4259840 | tf_op jit(solution)/shard_map/all_gather | solution.py:51
  11.1 120.0 %copy-start.1 = (s32[8]{0:T(128)S(1)}, s32[8]{0:T(128)}, u32[]{:S(2)}) copy-start(s32[8]{0:T(128)} %param.13) | copy-start | bytes 100
  11.1 120.0 %all-to-all-start = ((bf16[64,256,128]{2,1,0:T(8,128)(2,1)}), bf16[64,256,128]{2,1,0:T(8,128)(2,1)}, u32[]{:S(2)}, u32[]{:S(2)}) async-start(bf16[64,256,128]{2,1,0:T(8,128)(2,1)} %tile.2), calls=%async_computation | async-start | bytes 8388608 | tf_op jit(solution)/shard_map/all_to_all | solution.py:46
  24.4 387.5 %all-gather.5.cloned.1.call-start = ((), (), s32[]{:S(2)}) async-start(), calls=%async_computation.2 | async-start | bytes 10485760 | tf_op jit(solution)/shard_map/all_gather | solution.py:15
  143.4 3.2 copy-start
  168.0 3.2 copy-start
  192.6 3.2 copy-start
  217.1 3.2 copy-start
  241.7 3.2 copy-start
  266.2 3.2 copy-start
  290.8 3.2 copy-start
  315.4 3.2 copy-start
Sparse Core Ops, SparseCore 0:
  10.1 104.3 all-gather.2
  327.8 84.0 all-gather.4
